TPU v7x, 256 devices: a whole 4x4x8 slice. The times are simulated.
256 devices in a mesh: dp: 16 (over z_lo, y, core), shard: 16 (over z_hi, x).
Axes of the slice: x: 4, y: 4, z: 8 (z_hi: 4, z_lo: 2; z = z_hi * 2 + z_lo), core: 2. Of those that a mesh axis runs over, the one named last changes fastest.
Arguments:
- grads: bfloat16 [16, 18, 7168, 128], P('dp', None, 'shard'), may hold values from -230 to 230
- params: float32 [18, 7168, 128], P(None, 'shard'), may hold values from -6 to 6
- table: int32 [18], replicated, may hold values from 0 to 17, each once
Outputs:
- new_params: float32 [18, 7168, 128], P(None, 'shard')
- update: bfloat16 [18, 7168, 128], P(None, 'shard')
Inputs may be any that keep to these rules, and one draw needn't show every extreme that they name: A permutation: gradient block j belongs to head table[j].
All inputs are finite; a program needn't handle non-finite values.
Results may differ from a plain program's by a relative error of at most 0.006.
Values may be sent and summed in bfloat16 or wider, within the bound.
A program may use at most 64 MiB of HBM per device.

v0:
```python
import functools
import math

import jax
import jax.numpy as jnp
from jax import lax
from jax.experimental import pallas as pl
from jax.experimental.pallas import tpu as pltpu
from jax.sharding import PartitionSpec as P

D = 7168
V = 128
HALF = V // 2
PACKED = HALF + 8
ITERS = 5
N_DP = 16
CHIPS = 8
TAIL_OWNERS = 7
CODE_MAX = 32767.0

quintic_one = 3.4445
quintic_two = -4.775
quintic_three = 2.0315
epsilon = 1e-07
learning_rate = 0.02
decay_rate = 0.1

MESH = pl.DeviceIdType.MESH
HIGHEST = lax.Precision.HIGHEST


def exact_dot(left, right):
    return jnp.dot(left, right, precision=HIGHEST, preferred_element_type=jnp.float32)


def places(rows):
    return (
        lax.broadcasted_iota(jnp.int32, (rows, V), 0),
        lax.broadcasted_iota(jnp.int32, (rows, V), 1),
    )


def gram_of(rows):
    return lax.dot_general(
        rows, rows, (((0,), (0,)), ((), ())), preferred_element_type=jnp.float32
    )


def pack(matrix):
    row, col = places(HALF)
    corner = pltpu.roll(matrix[HALF:], HALF, 1)
    body = jnp.where((col < HALF) & (row > col), corner, matrix[:HALF])
    diagonal = jnp.sum(jnp.where(row == col, corner, 0.0), axis=0, keepdims=True)
    return jnp.concatenate([body, jnp.broadcast_to(diagonal, (8, V))], axis=0)


def unpack(packed):
    row, col = places(HALF)
    body, diagonal = packed[:HALF], packed[HALF:HALF + 1]
    turned = jnp.concatenate([body, jnp.zeros_like(body)], axis=0).T
    top = jnp.where((col < HALF) & (row > col), turned[:HALF], body)
    corner = jnp.where(row > col, body, jnp.where(row < col, turned[:HALF], diagonal))
    bottom = jnp.where(col < HALF, turned[HALF:], pltpu.roll(corner, HALF, 1))
    return jnp.concatenate([top, bottom], axis=0)


def polynomial_of(total_gram, between):
    row, col = places(V)
    eye = (row == col).astype(jnp.float32)
    square = jnp.sum(jnp.sum(total_gram * eye, axis=1, keepdims=True), axis=0, keepdims=True)
    inverse = 1.0 / (jnp.sqrt(square) + epsilon)
    gram = (total_gram * inverse) * inverse
    product = None
    for index in range(ITERS):
        step = quintic_one * eye + quintic_two * gram + quintic_three * exact_dot(gram, gram)
        if index == ITERS - 1:
            product = exact_dot(product, step)
        elif index == 0:
            product = step
            gram = exact_dot(exact_dot(gram, step), step)
        else:
            both = exact_dot(jnp.concatenate([gram, product], axis=0), step)
            product = both[V:]
            gram = exact_dot(both[:V], step)
        between(index)
    return product * inverse


def coded(total):
    peak = jnp.maximum(jnp.max(jnp.abs(total), axis=0, keepdims=True), 1e-33)
    codes = jnp.round(total * (CODE_MAX / peak)).astype(jnp.int32).astype(jnp.int16)
    return codes, jnp.broadcast_to(peak * (1.0 / CODE_MAX), (8, V))


def decoded(codes, scale):
    return codes.astype(jnp.int32).astype(jnp.float32) * scale


def applied(block, packed):
    matrix = unpack(packed)
    high = matrix.astype(jnp.bfloat16)
    low = (matrix - high.astype(jnp.float32)).astype(jnp.bfloat16)
    return jnp.dot(
        jnp.concatenate([block, block], axis=1),
        jnp.concatenate([high, low], axis=0),
        preferred_element_type=jnp.float32,
    ).astype(jnp.bfloat16)


def communicate(
    grads, params, ortho, held_params,
    mine, theirs, codes, scales, got_codes, got_scales,
    tail_codes, tail_scales, got_tail, got_tail_scales,
    x, p, total, sums, from_x, from_z,
    mine_sems, their_sems, their_send, code_sems, scale_sems, code_send, scale_send,
    tail_sem, tail_scale_sem, tail_send, tail_scale_send, tailx_sem, tailx_send, tails_sem, tails_send,
    gx_sems, gx_send, gz_sems, gz_send, x_sems, x_send, p_sems, p_send, tailp_sem, params_sem,
    *, count, rows,
):
    piece = rows // TAIL_OWNERS
    me = lax.axis_index("dp")
    shard = lax.axis_index("shard")
    core = lax.rem(me, 2)
    chip = me // 2
    sibling = me + 1 - 2 * core
    tail_block = N_DP + core
    tail_other = N_DP + 1 - core

    def chip_at(offset, sign=1):
        z = lax.rem(chip // 4 + offset // 4, 2)
        y = lax.rem(lax.rem(chip, 4) + 4 + sign * (offset % 4), 4)
        return 4 * z + y

    def to(offset):
        return 2 * chip_at(offset) + core

    def source(offset):
        return 2 * chip_at(offset, -1) + core

    def rows_of(block):
        return pl.ds(block * rows, rows)

    def x_peer(step):
        return shard - lax.rem(shard, 4) + lax.rem(lax.rem(shard, 4) + step, 4)

    def z_peer(step):
        return lax.rem(shard // 4 + step, 4) * 4 + lax.rem(shard, 4)

    def remote(src, dst, send_sem, recv_sem, **device):
        pltpu.make_async_remote_copy(
            src_ref=src, dst_ref=dst, send_sem=send_sem, recv_sem=recv_sem,
            device_id=device, device_id_type=MESH,
        ).start()

    def finished(ref, sem):
        pltpu.make_async_copy(ref, ref, sem).wait()

    order = (6, 2, 5, 7, 4, 1, 3)

    barrier = pltpu.get_barrier_semaphore()
    for offset in range(1, CHIPS):
        pl.semaphore_signal(barrier, inc=1, device_id={"dp": to(offset)}, device_id_type=MESH)
    pl.semaphore_signal(barrier, inc=1, device_id={"dp": sibling}, device_id_type=MESH)
    for step in range(1, 4):
        pl.semaphore_signal(barrier, inc=1, device_id={"shard": x_peer(step)}, device_id_type=MESH)
        pl.semaphore_signal(barrier, inc=1, device_id={"shard": z_peer(step)}, device_id_type=MESH)

    pltpu.make_async_copy(grads.at[rows_of(tail_block)], mine.at[CHIPS], mine_sems.at[CHIPS]).start()
    for offset in order + (0,):
        pltpu.make_async_copy(
            grads.at[rows_of(to(offset))], mine.at[offset], mine_sems.at[offset]
        ).start()
    pl.semaphore_wait(barrier, CHIPS + 6)
    remote(grads.at[rows_of(tail_other)], theirs.at[CHIPS], their_send, their_sems.at[CHIPS], dp=sibling)
    for offset in order + (0,):
        remote(
            grads.at[rows_of(to(offset) + 1 - 2 * core)],
            theirs.at[offset],
            their_send,
            their_sems.at[offset],
            dp=sibling,
        )
    keep_params = pltpu.make_async_copy(params, held_params, params_sem)
    keep_params.start()

    def pair_sum(slot):
        finished(mine.at[slot], mine_sems.at[slot])
        finished(theirs.at[slot], their_sems.at[slot])
        return mine[slot].astype(jnp.float32) + theirs[slot].astype(jnp.float32)

    pair = pair_sum(CHIPS)
    packed, scale = coded(pair)
    tail_codes[...] = packed
    tail_scales[...] = scale
    for offset in order:
        peer = chip_at(offset)

        @pl.when(peer < TAIL_OWNERS)
        def _():
            remote(
                tail_codes.at[pl.ds(peer * piece, piece)], got_tail.at[offset], tail_send, tail_sem,
                dp=2 * peer + core,
            )
            remote(tail_scales, got_tail_scales.at[offset], tail_scale_send, tail_scale_sem, dp=2 * peer + core)

    def send_codes(offset):
        packed, scale = coded(pair_sum(offset))
        codes[offset] = packed
        scales[offset] = scale
        remote(codes.at[offset], got_codes.at[offset], code_send, code_sems.at[offset], dp=to(offset))
        remote(scales.at[offset], got_scales.at[offset], scale_send, scale_sems.at[offset], dp=to(offset))

    for offset in order[:4]:
        send_codes(offset)

    tail_rows = pl.ds(tail_block * rows + chip * piece, piece)

    @pl.when(chip < TAIL_OWNERS)
    def _():
        here = pl.ds(pl.multiple_of(chip * piece, piece), piece)
        summed = mine[CHIPS, here].astype(jnp.float32) + theirs[CHIPS, here].astype(jnp.float32)
        finished(got_tail.at[pl.ds(1, CHIPS - 1)], tail_sem)
        finished(got_tail_scales.at[pl.ds(1, CHIPS - 1)], tail_scale_sem)
        for offset in range(1, CHIPS):
            summed = summed + decoded(got_tail[offset], got_tail_scales[offset, 0:1])
        x[tail_rows] = summed.astype(jnp.bfloat16)
        for offset in order:
            remote(x.at[tail_rows], x.at[tail_rows], tailx_send, tailx_sem, dp=to(offset))

    for offset in order[4:]:
        send_codes(offset)
    total[...] = pair_sum(0)

    @pl.when(chip < TAIL_OWNERS)
    def _():
        finished(got_tail.at[pl.ds(0, TAIL_OWNERS - 1)], tailx_sem)

    @pl.when(chip >= TAIL_OWNERS)
    def _():
        finished(got_tail.at[pl.ds(0, TAIL_OWNERS)], tailx_sem)

    remote(x.at[rows_of(tail_block)], x.at[rows_of(tail_block)], tails_send, tails_sem, dp=sibling)

    def start_x(which, gram):
        sums[which, 0] = pack(gram)
        for step in (2, 1, 3):
            remote(
                sums.at[which, 0], from_x.at[which, step - 1], gx_send.at[which], gx_sems.at[which],
                shard=x_peer(step),
            )

    def start_z(which):
        finished(from_x.at[which], gx_sems.at[which])
        sums[which, 1] = sums[which, 0] + from_x[which, 0] + from_x[which, 1] + from_x[which, 2]
        for step in (2, 1, 3):
            remote(
                sums.at[which, 1], from_z.at[which, step - 1], gz_send.at[which], gz_sems.at[which],
                shard=z_peer(step),
            )

    def total_gram(which):
        finished(from_z.at[which], gz_sems.at[which])
        return unpack(sums[which, 1] + from_z[which, 0] + from_z[which, 1] + from_z[which, 2])

    start_x(0, gram_of(x[rows_of(tail_block)]))

    for offset in order:
        finished(got_codes.at[offset], code_sems.at[offset])
        finished(got_scales.at[offset], scale_sems.at[offset])
        total[...] = total[...] + decoded(got_codes[offset], got_scales[offset, 0:1])
    here = x.at[rows_of(me)]
    x[rows_of(me)] = total[...].astype(jnp.bfloat16)
    start_x(1, gram_of(x[rows_of(me)]))
    start_z(0)

    for offset in (2, 1, 3):
        remote(here, here, x_send, x_sems.at[offset], dp=to(offset))
    remote(here, here, x_send, x_sems.at[0], dp=sibling)
    start_z(1)
    remote(here, here, x_send, x_sems.at[4], dp=to(4))

    def pass_x(offset):
        place = x.at[rows_of(source(offset))]
        finished(place, x_sems.at[offset])
        remote(place, place, x_send, x_sems.at[CHIPS + offset], dp=sibling)
        if offset == 4:
            for step in (2, 1, 3):
                remote(place, place, x_send, x_sems.at[4 + step], dp=to(step))

    def between_tail(index):
        for offset in ((), (1,), (3,), (2,), (4,))[index]:
            pass_x(offset)

    p[tail_block] = pack(polynomial_of(total_gram(0), between_tail))
    remote(p.at[tail_block], p.at[tail_block], p_send, tailp_sem, dp=sibling)
    ortho[rows_of(tail_block)] = applied(x[rows_of(tail_block)], p[tail_block])

    def between_own(index):
        for offset in ((), (), (5,), (7,), (6,))[index]:
            pass_x(offset)

    p[me] = pack(polynomial_of(total_gram(1), between_own))
    for offset in order:
        remote(p.at[me], p.at[me], p_send, p_sems.at[offset], dp=to(offset))
    remote(p.at[me], p.at[me], p_send, p_sems.at[0], dp=sibling)

    def apply_at(block):
        ortho[rows_of(block)] = applied(x[rows_of(block)], p[block])

    apply_at(me)
    finished(x.at[rows_of(tail_other)], tails_sem)
    finished(p.at[tail_other], tailp_sem)
    apply_at(tail_other)
    finished(x.at[rows_of(sibling)], x_sems.at[0])
    finished(p.at[sibling], p_sems.at[0])
    apply_at(sibling)

    for offset in (4, 1, 3, 5, 7, 2, 6):
        place = p.at[source(offset)]
        finished(place, p_sems.at[offset])
        remote(place, place, p_send, p_sems.at[CHIPS + offset], dp=sibling)
        apply_at(source(offset))
    for offset in (4, 1, 3, 5, 7, 2, 6):
        other = source(offset) + 1 - 2 * core
        finished(x.at[rows_of(other)], x_sems.at[CHIPS + offset])
        finished(p.at[other], p_sems.at[CHIPS + offset])
        apply_at(other)

    keep_params.wait()
    finished(theirs, their_send)
    finished(got_codes.at[pl.ds(1, CHIPS - 1)], code_send)
    finished(got_scales.at[pl.ds(1, CHIPS - 1)], scale_send)

    @pl.when(chip < TAIL_OWNERS)
    def _():
        finished(got_tail.at[pl.ds(0, TAIL_OWNERS - 1)], tail_send)
        finished(got_tail_scales.at[pl.ds(0, TAIL_OWNERS - 1)], tail_scale_send)
        finished(got_tail.at[pl.ds(0, CHIPS - 1)], tailx_send)

    @pl.when(chip >= TAIL_OWNERS)
    def _():
        finished(got_tail.at[pl.ds(0, TAIL_OWNERS)], tail_send)
        finished(got_tail_scales.at[pl.ds(0, TAIL_OWNERS)], tail_scale_send)

    finished(x.at[rows_of(tail_block)], tails_send)
    for which in range(2):
        finished(from_x.at[which], gx_send.at[which])
        finished(from_z.at[which], gz_send.at[which])
    finished(x.at[pl.ds(0, 15 * rows)], x_send)
    finished(p.at[pl.ds(0, 16)], p_send)


def exchange(grads, params, count, rows):
    piece = rows // TAIL_OWNERS
    dma = pltpu.SemaphoreType.DMA
    vmem = pltpu.VMEM
    return pl.pallas_call(
        functools.partial(communicate, count=count, rows=rows),
        out_shape=(
            jax.ShapeDtypeStruct((count * rows, V), jnp.bfloat16),
            jax.ShapeDtypeStruct((count * rows, V), jnp.float32),
        ),
        in_specs=[pl.BlockSpec(memory_space=pltpu.HBM)] * 2,
        out_specs=(pl.BlockSpec(memory_space=vmem), pl.BlockSpec(memory_space=vmem)),
        scratch_shapes=[
            vmem((CHIPS + 1, rows, V), jnp.bfloat16),
            vmem((CHIPS + 1, rows, V), jnp.bfloat16),
            vmem((CHIPS, rows, V), jnp.int16),
            vmem((CHIPS, 8, V), jnp.float32),
            vmem((CHIPS, rows, V), jnp.int16),
            vmem((CHIPS, 8, V), jnp.float32),
            vmem((rows, V), jnp.int16),
            vmem((8, V), jnp.float32),
            vmem((CHIPS, piece, V), jnp.int16),
            vmem((CHIPS, 8, V), jnp.float32),
            vmem((count * rows, V), jnp.bfloat16),
            vmem((count, PACKED, V), jnp.float32),
            vmem((rows, V), jnp.float32),
            vmem((2, 2, PACKED, V), jnp.float32),
            vmem((2, 3, PACKED, V), jnp.float32),
            vmem((2, 3, PACKED, V), jnp.float32),
            dma((CHIPS + 1,)), dma((CHIPS + 1,)), dma, dma((CHIPS,)), dma((CHIPS,)), dma, dma,
            dma, dma, dma, dma, dma, dma, dma, dma,
            dma((2,)), dma((2,)), dma((2,)), dma((2,)),
            dma((2 * CHIPS,)), dma, dma((2 * CHIPS,)), dma, dma, dma,
        ],
        compiler_params=pltpu.CompilerParams(
            collective_id=0, has_side_effects=True, vmem_limit_bytes=40 * 2**20
        ),
    )(grads, params)


def finish(table, ortho, params, new_params, update, new_held, update_held, sems):
    count = ortho.shape[0]

    def one(j, carry):
        head = table[j]
        scaled = 0.2 * math.sqrt(max(D, V)) * ortho[j].astype(jnp.float32)
        old = params[head]
        new_held[j] = old - learning_rate * (scaled + decay_rate * old)
        update_held[j] = scaled.astype(jnp.bfloat16)
        pltpu.make_async_copy(new_held.at[j], new_params.at[head], sems.at[0]).start()
        pltpu.make_async_copy(update_held.at[j], update.at[head], sems.at[1]).start()
        return carry

    lax.fori_loop(0, count, one, 0)
    pltpu.make_async_copy(new_held, new_params, sems.at[0]).wait()
    pltpu.make_async_copy(update_held, update, sems.at[1]).wait()


def apply(table, ortho, params):
    vmem = pltpu.VMEM
    return pl.pallas_call(
        finish,
        in_specs=[
            pl.BlockSpec(memory_space=pltpu.SMEM),
            pl.BlockSpec(memory_space=vmem),
            pl.BlockSpec(memory_space=vmem),
        ],
        out_specs=(pl.BlockSpec(memory_space=pltpu.HBM), pl.BlockSpec(memory_space=pltpu.HBM)),
        out_shape=(
            jax.ShapeDtypeStruct(params.shape, jnp.float32),
            jax.ShapeDtypeStruct(params.shape, jnp.bfloat16),
        ),
        scratch_shapes=[
            vmem(params.shape, jnp.float32),
            vmem(params.shape, jnp.bfloat16),
            pltpu.SemaphoreType.DMA((2,)),
        ],
        compiler_params=pltpu.CompilerParams(vmem_limit_bytes=32 * 2**20),
    )(table, ortho, params)


def per_device(grads, params, table):
    count, rows, width = params.shape
    flat = (count * rows, width)
    ortho, held = exchange(pltpu.with_memory_space_constraint(grads.reshape(flat), pltpu.HBM), pltpu.with_memory_space_constraint(params.reshape(flat), pltpu.HBM), count, rows)
    return apply(table, ortho.reshape(params.shape), held.reshape(params.shape))


def solution(mesh):
    return jax.shard_map(
        per_device,
        mesh=mesh,
        in_specs=(P("dp", None, "shard", None), P(None, "shard", None), P()),
        out_specs=(P(None, "shard", None), P(None, "shard", None)),
        check_vma=False,
    )
```

profile of v0, /device:TPU:1, one launch (start us, length us, event | category | flops | bytes accessed | tf_op | source)
XLA Modules:
  0.0 64.9 jit_solution(9979043334497139249)
XLA Ops:
  0.6 0.0 copy-start
  0.6 61.0 %shard_map.50 = (bf16[8064,128]{1,0:T(8,128)(2,1)S(1)}, f32[8064,128]{1,0:T(8,128)S(1)}) custom-call(bf16[8064,128]{1,0:T(8,128)(2,1)} %bitcast.7, f32[8064,128]{1,0:T(8,128)} %bitcast.6), custom_call_target="tpu_custom_call" | custom-call | tf_op jit(solution)/shard_map/pallas_call | solution.py:357
  61.7 0.0 copy-done
  61.7 3.2 %shard_map.51 = (f32[18,448,128]{2,1,0:T(8,128)}, bf16[18,448,128]{2,1,0:T(8,128)(2,1)}) custom-call(s32[18]{0:T(128)S(1)} %copy-done, bf16[18,448,128]{2,1,0:T(8,128)(2,1)S(1)} %bitcast.5, f32[18,448,128]{2,1,0:T(8,128)S(1)} %bitcast.4), custom_call_target="tpu_custom_call" | custom-call | tf_op jit(solution)/shard_map/pallas_call | solution.py:413
Async XLA Ops:
  0.6 61.0 %copy-start = (s32[18]{0:T(128)S(1)}, s32[18]{0:T(128)}, u32[]{:S(2)}) copy-start(s32[18]{0:T(128)} %table.1) | copy-start | bytes 220
where the time goes:
time: 64.9 us
  Pallas kernels  64.2 us (99%)
  between operations  0.65 us (1%)
    pallas_call x1, Pallas kernels, exchange(): pl.pallas_call(functools.partial(communicate, count=count, rows=rows), ou...  61 us
    pallas_call x1, Pallas kernels, apply(): pl.pallas_call(finish, in_specs=[pl.BlockSpec(memory_space=pltpu.SMEM), p...  3.2 us

commit v1 on v0

--- a/solution.py
+++ b/solution.py
@@ -114,7 +114,7 @@
     x, p, total, sums, from_x, from_z,
     mine_sems, their_sems, their_send, code_sems, scale_sems, code_send, scale_send,
     tail_sem, tail_scale_sem, tail_send, tail_scale_send, tailx_sem, tailx_send, tails_sem, tails_send,
-    gx_sems, gx_send, gz_sems, gz_send, x_sems, x_send, p_sems, p_send, tailp_sem, params_sem,
+    gx_sems, gx_send, gz_sems, gz_send, x_sems, z_sems, x_send, p_sems, p_send, tailp_sem, params_sem,
     *, count, rows,
 ):
     piece = rows // TAIL_OWNERS
@@ -203,15 +203,20 @@
             )
             remote(tail_scales, got_tail_scales.at[offset], tail_scale_send, tail_scale_sem, dp=2 * peer + core)
 
-    def send_codes(offset):
+    halves = (pl.ds(0, rows // 2), pl.ds(rows // 2, rows // 2))
+
+    def send_codes(half, offset):
+        remote(
+            codes.at[offset, halves[half]], got_codes.at[offset, halves[half]], code_send,
+            code_sems.at[half, offset], dp=to(offset),
+        )
+
+    for offset in order:
         packed, scale = coded(pair_sum(offset))
         codes[offset] = packed
         scales[offset] = scale
-        remote(codes.at[offset], got_codes.at[offset], code_send, code_sems.at[offset], dp=to(offset))
         remote(scales.at[offset], got_scales.at[offset], scale_send, scale_sems.at[offset], dp=to(offset))
-
-    for offset in order[:4]:
-        send_codes(offset)
+        send_codes(0, offset)
 
     tail_rows = pl.ds(tail_block * rows + chip * piece, piece)
 
@@ -227,19 +232,9 @@
         for offset in order:
             remote(x.at[tail_rows], x.at[tail_rows], tailx_send, tailx_sem, dp=to(offset))
 
-    for offset in order[4:]:
-        send_codes(offset)
+    for offset in order:
+        send_codes(1, offset)
     total[...] = pair_sum(0)
-
-    @pl.when(chip < TAIL_OWNERS)
-    def _():
-        finished(got_tail.at[pl.ds(0, TAIL_OWNERS - 1)], tailx_sem)
-
-    @pl.when(chip >= TAIL_OWNERS)
-    def _():
-        finished(got_tail.at[pl.ds(0, TAIL_OWNERS)], tailx_sem)
-
-    remote(x.at[rows_of(tail_block)], x.at[rows_of(tail_block)], tails_send, tails_sem, dp=sibling)
 
     def start_x(which, gram):
         sums[which, 0] = pack(gram)
@@ -262,30 +257,57 @@
         finished(from_z.at[which], gz_sems.at[which])
         return unpack(sums[which, 1] + from_z[which, 0] + from_z[which, 1] + from_z[which, 2])
 
-    start_x(0, gram_of(x[rows_of(tail_block)]))
-
-    for offset in order:
-        finished(got_codes.at[offset], code_sems.at[offset])
-        finished(got_scales.at[offset], scale_sems.at[offset])
-        total[...] = total[...] + decoded(got_codes[offset], got_scales[offset, 0:1])
-    here = x.at[rows_of(me)]
-    x[rows_of(me)] = total[...].astype(jnp.bfloat16)
-    start_x(1, gram_of(x[rows_of(me)]))
-    start_z(0)
-
-    for offset in (2, 1, 3):
-        remote(here, here, x_send, x_sems.at[offset], dp=to(offset))
-    remote(here, here, x_send, x_sems.at[0], dp=sibling)
-    start_z(1)
-    remote(here, here, x_send, x_sems.at[4], dp=to(4))
+    def own_half(half):
+        here = halves[half]
+        for offset in order:
+            finished(got_codes.at[offset, here], code_sems.at[half, offset])
+            if half == 0:
+                finished(got_scales.at[offset], scale_sems.at[offset])
+            total[here] = total[here] + decoded(got_codes[offset, here], got_scales[offset, 0:1])
+        summed = total[here].astype(jnp.bfloat16)
+        x[pl.ds(me * rows + half * (rows // 2), rows // 2)] = summed
+        return gram_of(summed)
+
+    def spread_half(half):
+        place = x.at[pl.ds(me * rows + half * (rows // 2), rows // 2)]
+        remote(place, place, x_send, z_sems.at[half], dp=to(4))
+        for offset in (2, 1, 3):
+            remote(place, place, x_send, x_sems.at[offset], dp=to(offset))
+        remote(place, place, x_send, x_sems.at[0], dp=sibling)
+
+    def pass_half(half):
+        place = x.at[pl.ds(source(4) * rows + half * (rows // 2), rows // 2)]
+        finished(place, z_sems.at[half])
+        for step in (2, 1, 3):
+            remote(place, place, x_send, x_sems.at[4 + step], dp=to(step))
 
     def pass_x(offset):
         place = x.at[rows_of(source(offset))]
-        finished(place, x_sems.at[offset])
+        if offset != 4:
+            finished(place, x_sems.at[offset])
         remote(place, place, x_send, x_sems.at[CHIPS + offset], dp=sibling)
-        if offset == 4:
-            for step in (2, 1, 3):
-                remote(place, place, x_send, x_sems.at[4 + step], dp=to(step))
+
+    first_gram = own_half(0)
+    spread_half(0)
+
+    @pl.when(chip < TAIL_OWNERS)
+    def _():
+        finished(got_tail.at[pl.ds(0, TAIL_OWNERS - 1)], tailx_sem)
+
+    @pl.when(chip >= TAIL_OWNERS)
+    def _():
+        finished(got_tail.at[pl.ds(0, TAIL_OWNERS)], tailx_sem)
+
+    remote(x.at[rows_of(tail_block)], x.at[rows_of(tail_block)], tails_send, tails_sem, dp=sibling)
+
+    start_x(0, gram_of(x[rows_of(tail_block)]))
+    start_z(0)
+
+    start_x(1, own_half(1) + first_gram)
+    spread_half(1)
+    pass_half(0)
+    start_z(1)
+    pass_half(1)
 
     def between_tail(index):
         for offset in ((), (1,), (3,), (2,), (4,))[index]:
@@ -295,11 +317,7 @@
     remote(p.at[tail_block], p.at[tail_block], p_send, tailp_sem, dp=sibling)
     ortho[rows_of(tail_block)] = applied(x[rows_of(tail_block)], p[tail_block])
 
-    def between_own(index):
-        for offset in ((), (), (5,), (7,), (6,))[index]:
-            pass_x(offset)
-
-    p[me] = pack(polynomial_of(total_gram(1), between_own))
+    p[me] = pack(polynomial_of(total_gram(1), lambda index: None))
     for offset in order:
         remote(p.at[me], p.at[me], p_send, p_sems.at[offset], dp=to(offset))
     remote(p.at[me], p.at[me], p_send, p_sems.at[0], dp=sibling)
@@ -308,6 +326,8 @@
         ortho[rows_of(block)] = applied(x[rows_of(block)], p[block])
 
     apply_at(me)
+    for offset in (5, 7, 6):
+        pass_x(offset)
     finished(x.at[rows_of(tail_other)], tails_sem)
     finished(p.at[tail_other], tailp_sem)
     apply_at(tail_other)
@@ -379,10 +399,10 @@
             vmem((2, 2, PACKED, V), jnp.float32),
             vmem((2, 3, PACKED, V), jnp.float32),
             vmem((2, 3, PACKED, V), jnp.float32),
-            dma((CHIPS + 1,)), dma((CHIPS + 1,)), dma, dma((CHIPS,)), dma((CHIPS,)), dma, dma,
+            dma((CHIPS + 1,)), dma((CHIPS + 1,)), dma, dma((2, CHIPS)), dma((CHIPS,)), dma, dma,
             dma, dma, dma, dma, dma, dma, dma, dma,
             dma((2,)), dma((2,)), dma((2,)), dma((2,)),
-            dma((2 * CHIPS,)), dma, dma((2 * CHIPS,)), dma, dma, dma,
+            dma((2 * CHIPS,)), dma((2,)), dma, dma((2 * CHIPS,)), dma, dma, dma,
         ],
         compiler_params=pltpu.CompilerParams(
             collective_id=0, has_side_effects=True, vmem_limit_bytes=40 * 2**20

time: 64.9 us -> 57.2 us (0.88)
  Pallas kernels: 64.2 us -> 56.5 us
    pallas_call x1, Pallas kernels: 61 us -> 53.3 us  [exchange(): pl.pallas_call(functools.partial(communicate, count=count, rows=rows), ou...]
where the time goes in v1:
time: 57.2 us
  Pallas kernels  56.5 us (99%)
  between operations  0.65 us (1%)
    pallas_call x1, Pallas kernels, exchange(): pl.pallas_call(functools.partial(communicate, count=count, rows=rows), ou...  53.3 us
    pallas_call x1, Pallas kernels, apply(): pl.pallas_call(finish, in_specs=[pl.BlockSpec(memory_space=pltpu.SMEM), p...  3.2 us

profile of v1, /device:TPU:1, one launch (start us, length us, event | category | flops | bytes accessed | tf_op | source)
XLA Modules:
  0.0 57.2 jit_solution(12700560702178077893)
XLA Ops:
  0.6 0.0 copy-start
  0.6 53.3 %shard_map.50 = (bf16[8064,128]{1,0:T(8,128)(2,1)S(1)}, f32[8064,128]{1,0:T(8,128)S(1)}) custom-call(bf16[8064,128]{1,0:T(8,128)(2,1)} %bitcast.7, f32[8064,128]{1,0:T(8,128)} %bitcast.6), custom_call_target="tpu_custom_call" | custom-call | tf_op jit(solution)/shard_map/pallas_call | solution.py:377
  54.0 0.0 copy-done
  54.0 3.2 %shard_map.51 = (f32[18,448,128]{2,1,0:T(8,128)}, bf16[18,448,128]{2,1,0:T(8,128)(2,1)}) custom-call(s32[18]{0:T(128)S(1)} %copy-done, bf16[18,448,128]{2,1,0:T(8,128)(2,1)S(1)} %bitcast.5, f32[18,448,128]{2,1,0:T(8,128)S(1)} %bitcast.4), custom_call_target="tpu_custom_call" | custom-call | tf_op jit(solution)/shard_map/pallas_call | solution.py:433
Async XLA Ops:
  0.6 53.3 %copy-start = (s32[18]{0:T(128)S(1)}, s32[18]{0:T(128)}, u32[]{:S(2)}) copy-start(s32[18]{0:T(128)} %table.1) | copy-start | bytes 220

commit v2 on v1

--- a/solution.py
+++ b/solution.py
@@ -12,6 +12,7 @@
 V = 128
 HALF = V // 2
 PACKED = HALF + 8
+QUARTER = HALF // 4
 ITERS = 5
 N_DP = 16
 CHIPS = 8
@@ -26,11 +27,10 @@
 decay_rate = 0.1
 
 MESH = pl.DeviceIdType.MESH
-HIGHEST = lax.Precision.HIGHEST
 
 
 def exact_dot(left, right):
-    return jnp.dot(left, right, precision=HIGHEST, preferred_element_type=jnp.float32)
+    return jnp.dot(left, right, precision=lax.Precision.HIGHEST, preferred_element_type=jnp.float32)
 
 
 def places(rows):
@@ -64,7 +64,7 @@
     return jnp.concatenate([top, bottom], axis=0)
 
 
-def polynomial_of(total_gram, between):
+def polynomial_of(total_gram):
     row, col = places(V)
     eye = (row == col).astype(jnp.float32)
     square = jnp.sum(jnp.sum(total_gram * eye, axis=1, keepdims=True), axis=0, keepdims=True)
@@ -82,7 +82,6 @@
             both = exact_dot(jnp.concatenate([gram, product], axis=0), step)
             product = both[V:]
             gram = exact_dot(both[:V], step)
-        between(index)
     return product * inverse
 
 
@@ -109,12 +108,12 @@
 
 def communicate(
     grads, params, ortho, held_params,
-    mine, theirs, codes, scales, got_codes, got_scales,
+    mine, given, theirs, codes, scales, got_codes, got_scales,
     tail_codes, tail_scales, got_tail, got_tail_scales,
-    x, p, total, sums, from_x, from_z,
-    mine_sems, their_sems, their_send, code_sems, scale_sems, code_send, scale_send,
+    x, p, total, parts, sums, quarters, from_x, from_z, whole, whole_x, whole_z,
+    mine_sems, given_sems, their_sems, their_send, code_sems, scale_sems, code_send, scale_send,
     tail_sem, tail_scale_sem, tail_send, tail_scale_send, tailx_sem, tailx_send, tails_sem, tails_send,
-    gx_sems, gx_send, gz_sems, gz_send, x_sems, z_sems, x_send, p_sems, p_send, tailp_sem, params_sem,
+    gx_sem, gx_send, gz_sem, gz_send, gq_sem, gq_send, wx_sem, wx_send, wz_sem, wz_send, x_sems, z_sems, x_send, p_sems, p_send, tailp_sem, params_sem,
     *, count, rows,
 ):
     piece = rows // TAIL_OWNERS
@@ -165,21 +164,18 @@
         pl.semaphore_signal(barrier, inc=1, device_id={"shard": x_peer(step)}, device_id_type=MESH)
         pl.semaphore_signal(barrier, inc=1, device_id={"shard": z_peer(step)}, device_id_type=MESH)
 
-    pltpu.make_async_copy(grads.at[rows_of(tail_block)], mine.at[CHIPS], mine_sems.at[CHIPS]).start()
-    for offset in order + (0,):
-        pltpu.make_async_copy(
-            grads.at[rows_of(to(offset))], mine.at[offset], mine_sems.at[offset]
-        ).start()
+    first_slots = ((CHIPS, tail_block, tail_other),) + tuple(
+        (offset, to(offset), to(offset) + 1 - 2 * core) for offset in order + (0,)
+    )
+    for slot, _, block in first_slots:
+        pltpu.make_async_copy(grads.at[rows_of(block)], given.at[slot], given_sems.at[slot]).start()
+    for slot, block, _ in first_slots:
+        pltpu.make_async_copy(grads.at[rows_of(block)], mine.at[slot], mine_sems.at[slot]).start()
+    for slot, _, _ in first_slots:
+        finished(given.at[slot], given_sems.at[slot])
     pl.semaphore_wait(barrier, CHIPS + 6)
-    remote(grads.at[rows_of(tail_other)], theirs.at[CHIPS], their_send, their_sems.at[CHIPS], dp=sibling)
-    for offset in order + (0,):
-        remote(
-            grads.at[rows_of(to(offset) + 1 - 2 * core)],
-            theirs.at[offset],
-            their_send,
-            their_sems.at[offset],
-            dp=sibling,
-        )
+    for slot, _, _ in first_slots:
+        remote(given.at[slot], theirs.at[slot], their_send, their_sems.at[slot], dp=sibling)
     keep_params = pltpu.make_async_copy(params, held_params, params_sem)
     keep_params.start()
 
@@ -236,26 +232,51 @@
         send_codes(1, offset)
     total[...] = pair_sum(0)
 
-    def start_x(which, gram):
-        sums[which, 0] = pack(gram)
+    across = lax.rem(shard, 4)
+
+    def tail_start_x(gram):
+        packed = pack(gram)
+        for quarter in range(4):
+            parts[quarter] = jnp.concatenate(
+                [packed[QUARTER * quarter:QUARTER * (quarter + 1)], packed[HALF:]], axis=0
+            )
         for step in (2, 1, 3):
             remote(
-                sums.at[which, 0], from_x.at[which, step - 1], gx_send.at[which], gx_sems.at[which],
+                parts.at[lax.rem(across + step, 4)], from_x.at[step - 1], gx_send, gx_sem,
                 shard=x_peer(step),
             )
 
-    def start_z(which):
-        finished(from_x.at[which], gx_sems.at[which])
-        sums[which, 1] = sums[which, 0] + from_x[which, 0] + from_x[which, 1] + from_x[which, 2]
+    def tail_start_z():
+        finished(from_x, gx_sem)
+        sums[...] = parts[across] + from_x[0] + from_x[1] + from_x[2]
         for step in (2, 1, 3):
-            remote(
-                sums.at[which, 1], from_z.at[which, step - 1], gz_send.at[which], gz_sems.at[which],
-                shard=z_peer(step),
-            )
-
-    def total_gram(which):
-        finished(from_z.at[which], gz_sems.at[which])
-        return unpack(sums[which, 1] + from_z[which, 0] + from_z[which, 1] + from_z[which, 2])
+            remote(sums, from_z.at[step - 1], gz_send, gz_sem, shard=z_peer(step))
+
+    def tail_start_quarters():
+        finished(from_z, gz_sem)
+        quarters[across] = sums[...] + from_z[0] + from_z[1] + from_z[2]
+        for step in (2, 1, 3):
+            remote(quarters.at[across], quarters.at[across], gq_send, gq_sem, shard=x_peer(step))
+
+    def tail_gram():
+        finished(from_x, gq_sem)
+        rows_in = [quarters[quarter, :QUARTER] for quarter in range(4)]
+        return unpack(jnp.concatenate(rows_in + [quarters[0, QUARTER:]], axis=0))
+
+    def start_x(gram):
+        whole[0] = pack(gram)
+        for step in (2, 1, 3):
+            remote(whole.at[0], whole_x.at[step - 1], wx_send, wx_sem, shard=x_peer(step))
+
+    def start_z():
+        finished(whole_x, wx_sem)
+        whole[1] = whole[0] + whole_x[0] + whole_x[1] + whole_x[2]
+        for step in (2, 1, 3):
+            remote(whole.at[1], whole_z.at[step - 1], wz_send, wz_sem, shard=z_peer(step))
+
+    def own_gram():
+        finished(whole_z, wz_sem)
+        return unpack(whole[1] + whole_z[0] + whole_z[1] + whole_z[2])
 
     def own_half(half):
         here = halves[half]
@@ -300,51 +321,59 @@
 
     remote(x.at[rows_of(tail_block)], x.at[rows_of(tail_block)], tails_send, tails_sem, dp=sibling)
 
-    start_x(0, gram_of(x[rows_of(tail_block)]))
-    start_z(0)
-
-    start_x(1, own_half(1) + first_gram)
+    tail_start_x(gram_of(x[rows_of(tail_block)]))
+    tail_start_z()
+
+    start_x(own_half(1) + first_gram)
     spread_half(1)
     pass_half(0)
-    start_z(1)
+    start_z()
     pass_half(1)
-
-    def between_tail(index):
-        for offset in ((), (1,), (3,), (2,), (4,))[index]:
-            pass_x(offset)
-
-    p[tail_block] = pack(polynomial_of(total_gram(0), between_tail))
-    remote(p.at[tail_block], p.at[tail_block], p_send, tailp_sem, dp=sibling)
-    ortho[rows_of(tail_block)] = applied(x[rows_of(tail_block)], p[tail_block])
-
-    p[me] = pack(polynomial_of(total_gram(1), lambda index: None))
-    for offset in order:
-        remote(p.at[me], p.at[me], p_send, p_sems.at[offset], dp=to(offset))
-    remote(p.at[me], p.at[me], p_send, p_sems.at[0], dp=sibling)
-
-    def apply_at(block):
-        ortho[rows_of(block)] = applied(x[rows_of(block)], p[block])
-
-    apply_at(me)
+    pass_x(4)
+    tail_start_quarters()
+    for offset in (1, 3, 2):
+        pass_x(offset)
+
+    def send_matrix(block, matrix):
+        p[block] = pack(matrix)
+        if block is me:
+            for offset in order:
+                remote(p.at[me], p.at[me], p_send, p_sems.at[offset], dp=to(offset))
+        remote(p.at[block], p.at[block], p_send, p_sems.at[0] if block is me else tailp_sem, dp=sibling)
+
+    send_matrix(me, polynomial_of(own_gram()))
     for offset in (5, 7, 6):
         pass_x(offset)
-    finished(x.at[rows_of(tail_other)], tails_sem)
-    finished(p.at[tail_other], tailp_sem)
-    apply_at(tail_other)
-    finished(x.at[rows_of(sibling)], x_sems.at[0])
-    finished(p.at[sibling], p_sems.at[0])
-    apply_at(sibling)
-
-    for offset in (4, 1, 3, 5, 7, 2, 6):
+    send_matrix(tail_block, polynomial_of(tail_gram()))
+
+    def apply_at(*blocks):
+        results = [applied(x[rows_of(block)], p[block]) for block in blocks]
+        for block, result in zip(blocks, results):
+            ortho[rows_of(block)] = result
+
+    def pass_p(offset):
         place = p.at[source(offset)]
         finished(place, p_sems.at[offset])
         remote(place, place, p_send, p_sems.at[CHIPS + offset], dp=sibling)
-        apply_at(source(offset))
+
+    def other_of(offset):
+        return source(offset) + 1 - 2 * core
+
+    finished(x.at[rows_of(sibling)], x_sems.at[0])
+    finished(p.at[sibling], p_sems.at[0])
+    for offset in (4, 1, 3):
+        pass_p(offset)
+    apply_at(me, sibling, source(4), source(1), source(3))
+    for offset in (5, 7, 2, 6):
+        pass_p(offset)
+    finished(x.at[rows_of(tail_other)], tails_sem)
+    finished(p.at[tail_other], tailp_sem)
+    apply_at(tail_block, tail_other, source(5), source(7), source(2), source(6))
     for offset in (4, 1, 3, 5, 7, 2, 6):
-        other = source(offset) + 1 - 2 * core
+        other = other_of(offset)
         finished(x.at[rows_of(other)], x_sems.at[CHIPS + offset])
         finished(p.at[other], p_sems.at[CHIPS + offset])
-        apply_at(other)
+    apply_at(*(other_of(offset) for offset in (4, 1, 3, 5, 7, 2, 6)))
 
     keep_params.wait()
     finished(theirs, their_send)
@@ -363,9 +392,11 @@
         finished(got_tail_scales.at[pl.ds(0, TAIL_OWNERS)], tail_scale_send)
 
     finished(x.at[rows_of(tail_block)], tails_send)
-    for which in range(2):
-        finished(from_x.at[which], gx_send.at[which])
-        finished(from_z.at[which], gz_send.at[which])
+    finished(from_x, gx_send)
+    finished(from_z, gz_send)
+    finished(from_x, gq_send)
+    finished(whole_x, wx_send)
+    finished(whole_z, wz_send)
     finished(x.at[pl.ds(0, 15 * rows)], x_send)
     finished(p.at[pl.ds(0, 16)], p_send)
 
@@ -385,6 +416,7 @@
         scratch_shapes=[
             vmem((CHIPS + 1, rows, V), jnp.bfloat16),
             vmem((CHIPS + 1, rows, V), jnp.bfloat16),
+            vmem((CHIPS + 1, rows, V), jnp.bfloat16),
             vmem((CHIPS, rows, V), jnp.int16),
             vmem((CHIPS, 8, V), jnp.float32),
             vmem((CHIPS, rows, V), jnp.int16),
@@ -396,12 +428,17 @@
             vmem((count * rows, V), jnp.bfloat16),
             vmem((count, PACKED, V), jnp.float32),
             vmem((rows, V), jnp.float32),
-            vmem((2, 2, PACKED, V), jnp.float32),
-            vmem((2, 3, PACKED, V), jnp.float32),
-            vmem((2, 3, PACKED, V), jnp.float32),
-            dma((CHIPS + 1,)), dma((CHIPS + 1,)), dma, dma((2, CHIPS)), dma((CHIPS,)), dma, dma,
+            vmem((4, QUARTER + 8, V), jnp.float32),
+            vmem((QUARTER + 8, V), jnp.float32),
+            vmem((4, QUARTER + 8, V), jnp.float32),
+            vmem((3, QUARTER + 8, V), jnp.float32),
+            vmem((3, QUARTER + 8, V), jnp.float32),
+            vmem((2, PACKED, V), jnp.float32),
+            vmem((3, PACKED, V), jnp.float32),
+            vmem((3, PACKED, V), jnp.float32),
+            dma((CHIPS + 1,)), dma((CHIPS + 1,)), dma((CHIPS + 1,)), dma, dma((2, CHIPS)), dma((CHIPS,)), dma, dma,
             dma, dma, dma, dma, dma, dma, dma, dma,
-            dma((2,)), dma((2,)), dma((2,)), dma((2,)),
+            dma, dma, dma, dma, dma, dma, dma, dma, dma, dma,
             dma((2 * CHIPS,)), dma((2,)), dma, dma((2 * CHIPS,)), dma, dma, dma,
         ],
         compiler_params=pltpu.CompilerParams(

time: 57.2 us -> 53.9 us (0.942)
  Pallas kernels: 56.5 us -> 53.2 us
    pallas_call x1, Pallas kernels: 53.3 us -> 50 us  [exchange(): pl.pallas_call(functools.partial(communicate, count=count, rows=rows), ou...]
where the time goes in v2:
time: 53.9 us; the launch traced here: 53.8 us
  Pallas kernels  53.2 us (99%)
  between operations  0.65 us (1%)
    pallas_call x1, Pallas kernels, exchange(): pl.pallas_call(functools.partial(communicate, count=count, rows=rows), ou...  50 us
    pallas_call x1, Pallas kernels, apply(): pl.pallas_call(finish, in_specs=[pl.BlockSpec(memory_space=pltpu.SMEM), p...  3.2 us

profile of v2, /device:TPU:1, one launch (start us, length us, event | category | flops | bytes accessed | tf_op | source)
XLA Modules:
  0.0 53.8 jit_solution(154898551942681353)
XLA Ops:
  0.6 0.0 copy-start
  0.6 50.0 %shard_map.50 = (bf16[8064,128]{1,0:T(8,128)(2,1)S(1)}, f32[8064,128]{1,0:T(8,128)S(1)}) custom-call(bf16[8064,128]{1,0:T(8,128)(2,1)} %bitcast.7, f32[8064,128]{1,0:T(8,128)} %bitcast.6), custom_call_target="tpu_custom_call" | custom-call | tf_op jit(solution)/shard_map/pallas_call | solution.py:408
  50.6 0.0 copy-done
  50.6 3.2 %shard_map.51 = (f32[18,448,128]{2,1,0:T(8,128)}, bf16[18,448,128]{2,1,0:T(8,128)(2,1)}) custom-call(s32[18]{0:T(128)S(1)} %copy-done, bf16[18,448,128]{2,1,0:T(8,128)(2,1)S(1)} %bitcast.5, f32[18,448,128]{2,1,0:T(8,128)S(1)} %bitcast.4), custom_call_target="tpu_custom_call" | custom-call | tf_op jit(solution)/shard_map/pallas_call | solution.py:470
Async XLA Ops:
  0.6 50.0 %copy-start = (s32[18]{0:T(128)S(1)}, s32[18]{0:T(128)}, u32[]{:S(2)}) copy-start(s32[18]{0:T(128)} %table.1) | copy-start | bytes 220

commit v3 on v2

--- a/solution.py
+++ b/solution.py
@@ -12,7 +12,6 @@
 V = 128
 HALF = V // 2
 PACKED = HALF + 8
-QUARTER = HALF // 4
 ITERS = 5
 N_DP = 16
 CHIPS = 8
@@ -110,10 +109,10 @@
     grads, params, ortho, held_params,
     mine, given, theirs, codes, scales, got_codes, got_scales,
     tail_codes, tail_scales, got_tail, got_tail_scales,
-    x, p, total, parts, sums, quarters, from_x, from_z, whole, whole_x, whole_z,
+    x, p, total, sums, from_x, from_z,
     mine_sems, given_sems, their_sems, their_send, code_sems, scale_sems, code_send, scale_send,
     tail_sem, tail_scale_sem, tail_send, tail_scale_send, tailx_sem, tailx_send, tails_sem, tails_send,
-    gx_sem, gx_send, gz_sem, gz_send, gq_sem, gq_send, wx_sem, wx_send, wz_sem, wz_send, x_sems, z_sems, x_send, p_sems, p_send, tailp_sem, params_sem,
+    gx_sems, gx_send, gz_sems, gz_send, x_sems, z_sems, x_send, p_sems, p_send, tailp_sem, params_sem,
     *, count, rows,
 ):
     piece = rows // TAIL_OWNERS
@@ -214,6 +213,9 @@
         remote(scales.at[offset], got_scales.at[offset], scale_send, scale_sems.at[offset], dp=to(offset))
         send_codes(0, offset)
 
+    for offset in order:
+        send_codes(1, offset)
+
     tail_rows = pl.ds(tail_block * rows + chip * piece, piece)
 
     @pl.when(chip < TAIL_OWNERS)
@@ -228,55 +230,28 @@
         for offset in order:
             remote(x.at[tail_rows], x.at[tail_rows], tailx_send, tailx_sem, dp=to(offset))
 
-    for offset in order:
-        send_codes(1, offset)
     total[...] = pair_sum(0)
 
-    across = lax.rem(shard, 4)
-
-    def tail_start_x(gram):
-        packed = pack(gram)
-        for quarter in range(4):
-            parts[quarter] = jnp.concatenate(
-                [packed[QUARTER * quarter:QUARTER * (quarter + 1)], packed[HALF:]], axis=0
-            )
+    def start_x(which, gram):
+        sums[which, 0] = pack(gram)
         for step in (2, 1, 3):
             remote(
-                parts.at[lax.rem(across + step, 4)], from_x.at[step - 1], gx_send, gx_sem,
+                sums.at[which, 0], from_x.at[which, step - 1], gx_send.at[which], gx_sems.at[which],
                 shard=x_peer(step),
             )
 
-    def tail_start_z():
-        finished(from_x, gx_sem)
-        sums[...] = parts[across] + from_x[0] + from_x[1] + from_x[2]
+    def start_z(which):
+        finished(from_x.at[which], gx_sems.at[which])
+        sums[which, 1] = sums[which, 0] + from_x[which, 0] + from_x[which, 1] + from_x[which, 2]
         for step in (2, 1, 3):
-            remote(sums, from_z.at[step - 1], gz_send, gz_sem, shard=z_peer(step))
-
-    def tail_start_quarters():
-        finished(from_z, gz_sem)
-        quarters[across] = sums[...] + from_z[0] + from_z[1] + from_z[2]
-        for step in (2, 1, 3):
-            remote(quarters.at[across], quarters.at[across], gq_send, gq_sem, shard=x_peer(step))
-
-    def tail_gram():
-        finished(from_x, gq_sem)
-        rows_in = [quarters[quarter, :QUARTER] for quarter in range(4)]
-        return unpack(jnp.concatenate(rows_in + [quarters[0, QUARTER:]], axis=0))
-
-    def start_x(gram):
-        whole[0] = pack(gram)
-        for step in (2, 1, 3):
-            remote(whole.at[0], whole_x.at[step - 1], wx_send, wx_sem, shard=x_peer(step))
-
-    def start_z():
-        finished(whole_x, wx_sem)
-        whole[1] = whole[0] + whole_x[0] + whole_x[1] + whole_x[2]
-        for step in (2, 1, 3):
-            remote(whole.at[1], whole_z.at[step - 1], wz_send, wz_sem, shard=z_peer(step))
-
-    def own_gram():
-        finished(whole_z, wz_sem)
-        return unpack(whole[1] + whole_z[0] + whole_z[1] + whole_z[2])
+            remote(
+                sums.at[which, 1], from_z.at[which, step - 1], gz_send.at[which], gz_sems.at[which],
+                shard=z_peer(step),
+            )
+
+    def total_gram(which):
+        finished(from_z.at[which], gz_sems.at[which])
+        return unpack(sums[which, 1] + from_z[which, 0] + from_z[which, 1] + from_z[which, 2])
 
     def own_half(half):
         here = halves[half]
@@ -310,6 +285,11 @@
 
     first_gram = own_half(0)
     spread_half(0)
+    start_x(1, own_half(1) + first_gram)
+    spread_half(1)
+    pass_half(0)
+    start_z(1)
+    pass_half(1)
 
     @pl.when(chip < TAIL_OWNERS)
     def _():
@@ -321,18 +301,11 @@
 
     remote(x.at[rows_of(tail_block)], x.at[rows_of(tail_block)], tails_send, tails_sem, dp=sibling)
 
-    tail_start_x(gram_of(x[rows_of(tail_block)]))
-    tail_start_z()
-
-    start_x(own_half(1) + first_gram)
-    spread_half(1)
-    pass_half(0)
-    start_z()
-    pass_half(1)
+    start_x(0, gram_of(x[rows_of(tail_block)]))
     pass_x(4)
-    tail_start_quarters()
     for offset in (1, 3, 2):
         pass_x(offset)
+    start_z(0)
 
     def send_matrix(block, matrix):
         p[block] = pack(matrix)
@@ -341,10 +314,10 @@
                 remote(p.at[me], p.at[me], p_send, p_sems.at[offset], dp=to(offset))
         remote(p.at[block], p.at[block], p_send, p_sems.at[0] if block is me else tailp_sem, dp=sibling)
 
-    send_matrix(me, polynomial_of(own_gram()))
+    send_matrix(me, polynomial_of(total_gram(1)))
     for offset in (5, 7, 6):
         pass_x(offset)
-    send_matrix(tail_block, polynomial_of(tail_gram()))
+    send_matrix(tail_block, polynomial_of(total_gram(0)))
 
     def apply_at(*blocks):
         results = [applied(x[rows_of(block)], p[block]) for block in blocks]
@@ -392,11 +365,9 @@
         finished(got_tail_scales.at[pl.ds(0, TAIL_OWNERS)], tail_scale_send)
 
     finished(x.at[rows_of(tail_block)], tails_send)
-    finished(from_x, gx_send)
-    finished(from_z, gz_send)
-    finished(from_x, gq_send)
-    finished(whole_x, wx_send)
-    finished(whole_z, wz_send)
+    for which in range(2):
+        finished(from_x.at[which], gx_send.at[which])
+        finished(from_z.at[which], gz_send.at[which])
     finished(x.at[pl.ds(0, 15 * rows)], x_send)
     finished(p.at[pl.ds(0, 16)], p_send)
 
@@ -428,17 +399,12 @@
             vmem((count * rows, V), jnp.bfloat16),
             vmem((count, PACKED, V), jnp.float32),
             vmem((rows, V), jnp.float32),
-            vmem((4, QUARTER + 8, V), jnp.float32),
-            vmem((QUARTER + 8, V), jnp.float32),
-            vmem((4, QUARTER + 8, V), jnp.float32),
-            vmem((3, QUARTER + 8, V), jnp.float32),
-            vmem((3, QUARTER + 8, V), jnp.float32),
-            vmem((2, PACKED, V), jnp.float32),
-            vmem((3, PACKED, V), jnp.float32),
-            vmem((3, PACKED, V), jnp.float32),
+            vmem((2, 2, PACKED, V), jnp.float32),
+            vmem((2, 3, PACKED, V), jnp.float32),
+            vmem((2, 3, PACKED, V), jnp.float32),
             dma((CHIPS + 1,)), dma((CHIPS + 1,)), dma((CHIPS + 1,)), dma, dma((2, CHIPS)), dma((CHIPS,)), dma, dma,
             dma, dma, dma, dma, dma, dma, dma, dma,
-            dma, dma, dma, dma, dma, dma, dma, dma, dma, dma,
+            dma((2,)), dma((2,)), dma((2,)), dma((2,)),
             dma((2 * CHIPS,)), dma((2,)), dma, dma((2 * CHIPS,)), dma, dma, dma,
         ],
         compiler_params=pltpu.CompilerParams(

time: 53.9 us -> 53 us (0.983)
  Pallas kernels: 53.2 us -> 52.2 us
    pallas_call x1, Pallas kernels: 50 us -> 49 us  [exchange(): pl.pallas_call(functools.partial(communicate, count=count, rows=rows), ou...]
where the time goes in v3:
time: 53 us; the launch traced here: 52.9 us
  Pallas kernels  52.2 us (98%)
  between operations  0.65 us (1%)
    pallas_call x1, Pallas kernels, exchange(): pl.pallas_call(functools.partial(communicate, count=count, rows=rows), ou...  49 us
    pallas_call x1, Pallas kernels, apply(): pl.pallas_call(finish, in_specs=[pl.BlockSpec(memory_space=pltpu.SMEM), p...  3.2 us

profile of v3, /device:TPU:1, one launch (start us, length us, event | category | flops | bytes accessed | tf_op | source)
XLA Modules:
  0.0 52.9 jit_solution(6646169410951545562)
XLA Ops:
  0.6 0.0 copy-start
  0.6 49.0 %shard_map.50 = (bf16[8064,128]{1,0:T(8,128)(2,1)S(1)}, f32[8064,128]{1,0:T(8,128)S(1)}) custom-call(bf16[8064,128]{1,0:T(8,128)(2,1)} %bitcast.7, f32[8064,128]{1,0:T(8,128)} %bitcast.6), custom_call_target="tpu_custom_call" | custom-call | tf_op jit(solution)/shard_map/pallas_call | solution.py:379
  49.7 0.0 copy-done
  49.7 3.2 %shard_map.51 = (f32[18,448,128]{2,1,0:T(8,128)}, bf16[18,448,128]{2,1,0:T(8,128)(2,1)}) custom-call(s32[18]{0:T(128)S(1)} %copy-done, bf16[18,448,128]{2,1,0:T(8,128)(2,1)S(1)} %bitcast.5, f32[18,448,128]{2,1,0:T(8,128)S(1)} %bitcast.4), custom_call_target="tpu_custom_call" | custom-call | tf_op jit(solution)/shard_map/pallas_call | solution.py:436
Async XLA Ops:
  0.6 49.1 %copy-start = (s32[18]{0:T(128)S(1)}, s32[18]{0:T(128)}, u32[]{:S(2)}) copy-start(s32[18]{0:T(128)} %table.1) | copy-start | bytes 220

commit v4 on v3

--- a/solution.py
+++ b/solution.py
@@ -28,8 +28,8 @@
 MESH = pl.DeviceIdType.MESH
 
 
-def exact_dot(left, right):
-    return jnp.dot(left, right, precision=lax.Precision.HIGHEST, preferred_element_type=jnp.float32)
+def exact_dot(left, right, precision=lax.Precision.HIGHEST):
+    return jnp.dot(left, right, precision=precision, preferred_element_type=jnp.float32)
 
 
 def places(rows):
@@ -71,16 +71,19 @@
     gram = (total_gram * inverse) * inverse
     product = None
     for index in range(ITERS):
-        step = quintic_one * eye + quintic_two * gram + quintic_three * exact_dot(gram, gram)
+        dot = functools.partial(
+            exact_dot, precision=lax.Precision.HIGHEST if index < ITERS - 2 else lax.Precision.HIGH
+        )
+        step = quintic_one * eye + quintic_two * gram + quintic_three * dot(gram, gram)
         if index == ITERS - 1:
-            product = exact_dot(product, step)
+            product = dot(product, step)
         elif index == 0:
             product = step
-            gram = exact_dot(exact_dot(gram, step), step)
+            gram = dot(dot(gram, step), step)
         else:
-            both = exact_dot(jnp.concatenate([gram, product], axis=0), step)
+            both = dot(jnp.concatenate([gram, product], axis=0), step)
             product = both[V:]
-            gram = exact_dot(both[:V], step)
+            gram = dot(both[:V], step)
     return product * inverse
 
 
@@ -156,12 +159,13 @@
     order = (6, 2, 5, 7, 4, 1, 3)
 
     barrier = pltpu.get_barrier_semaphore()
-    for offset in range(1, CHIPS):
+    for step in (2, 1, 3):
+        pl.semaphore_signal(barrier, inc=1, device_id={"shard": z_peer(step)}, device_id_type=MESH)
+    for offset in order:
         pl.semaphore_signal(barrier, inc=1, device_id={"dp": to(offset)}, device_id_type=MESH)
+    for step in (2, 1, 3):
+        pl.semaphore_signal(barrier, inc=1, device_id={"shard": x_peer(step)}, device_id_type=MESH)
     pl.semaphore_signal(barrier, inc=1, device_id={"dp": sibling}, device_id_type=MESH)
-    for step in range(1, 4):
-        pl.semaphore_signal(barrier, inc=1, device_id={"shard": x_peer(step)}, device_id_type=MESH)
-        pl.semaphore_signal(barrier, inc=1, device_id={"shard": z_peer(step)}, device_id_type=MESH)
 
     first_slots = ((CHIPS, tail_block, tail_other),) + tuple(
         (offset, to(offset), to(offset) + 1 - 2 * core) for offset in order + (0,)
@@ -232,25 +236,32 @@
 
     total[...] = pair_sum(0)
 
+    chunks = (pl.ds(0, HALF // 2), pl.ds(HALF // 2, PACKED - HALF // 2))
+
     def start_x(which, gram):
         sums[which, 0] = pack(gram)
-        for step in (2, 1, 3):
-            remote(
-                sums.at[which, 0], from_x.at[which, step - 1], gx_send.at[which], gx_sems.at[which],
-                shard=x_peer(step),
+        for index, part in enumerate(chunks):
+            for step in (2, 1, 3):
+                remote(
+                    sums.at[which, 0, part], from_x.at[which, step - 1, part], gx_send.at[which],
+                    gx_sems.at[which, index], shard=x_peer(step),
+                )
+
+    def start_z(which):
+        for index, part in enumerate(chunks):
+            finished(from_x.at[which, :, part], gx_sems.at[which, index])
+            sums[which, 1, part] = (
+                sums[which, 0, part] + from_x[which, 0, part] + from_x[which, 1, part] + from_x[which, 2, part]
             )
-
-    def start_z(which):
-        finished(from_x.at[which], gx_sems.at[which])
-        sums[which, 1] = sums[which, 0] + from_x[which, 0] + from_x[which, 1] + from_x[which, 2]
-        for step in (2, 1, 3):
-            remote(
-                sums.at[which, 1], from_z.at[which, step - 1], gz_send.at[which], gz_sems.at[which],
-                shard=z_peer(step),
-            )
+            for step in (2, 1, 3):
+                remote(
+                    sums.at[which, 1, part], from_z.at[which, step - 1, part], gz_send.at[which],
+                    gz_sems.at[which, index], shard=z_peer(step),
+                )
 
     def total_gram(which):
-        finished(from_z.at[which], gz_sems.at[which])
+        for index, part in enumerate(chunks):
+            finished(from_z.at[which, :, part], gz_sems.at[which, index])
         return unpack(sums[which, 1] + from_z[which, 0] + from_z[which, 1] + from_z[which, 2])
 
     def own_half(half):
@@ -404,7 +415,7 @@
             vmem((2, 3, PACKED, V), jnp.float32),
             dma((CHIPS + 1,)), dma((CHIPS + 1,)), dma((CHIPS + 1,)), dma, dma((2, CHIPS)), dma((CHIPS,)), dma, dma,
             dma, dma, dma, dma, dma, dma, dma, dma,
-            dma((2,)), dma((2,)), dma((2,)), dma((2,)),
+            dma((2, 2)), dma((2,)), dma((2, 2)), dma((2,)),
             dma((2 * CHIPS,)), dma((2,)), dma, dma((2 * CHIPS,)), dma, dma, dma,
         ],
         compiler_params=pltpu.CompilerParams(

time: 53 us -> 52.3 us (0.987)
  Pallas kernels: 52.2 us -> 51.6 us
    pallas_call x1, Pallas kernels: 49 us -> 48.4 us  [exchange(): pl.pallas_call(functools.partial(communicate, count=count, rows=rows), ou...]
where the time goes in v4:
time: 52.3 us; the launch traced here: 52.2 us
  Pallas kernels  51.6 us (99%)
  between operations  0.65 us (1%)
    pallas_call x1, Pallas kernels, exchange(): pl.pallas_call(functools.partial(communicate, count=count, rows=rows), ou...  48.4 us
    pallas_call x1, Pallas kernels, apply(): pl.pallas_call(finish, in_specs=[pl.BlockSpec(memory_space=pltpu.SMEM), p...  3.2 us

profile of v4, /device:TPU:1, one launch (start us, length us, event | category | flops | bytes accessed | tf_op | source)
XLA Modules:
  0.0 52.2 jit_solution(8560992970800336002)
XLA Ops:
  0.6 0.0 copy-start
  0.6 48.4 %shard_map.50 = (bf16[8064,128]{1,0:T(8,128)(2,1)S(1)}, f32[8064,128]{1,0:T(8,128)S(1)}) custom-call(bf16[8064,128]{1,0:T(8,128)(2,1)} %bitcast.7, f32[8064,128]{1,0:T(8,128)} %bitcast.6), custom_call_target="tpu_custom_call" | custom-call | tf_op jit(solution)/shard_map/pallas_call | solution.py:390
  49.0 0.0 copy-done
  49.0 3.2 %shard_map.51 = (f32[18,448,128]{2,1,0:T(8,128)}, bf16[18,448,128]{2,1,0:T(8,128)(2,1)}) custom-call(s32[18]{0:T(128)S(1)} %copy-done, bf16[18,448,128]{2,1,0:T(8,128)(2,1)S(1)} %bitcast.5, f32[18,448,128]{2,1,0:T(8,128)S(1)} %bitcast.4), custom_call_target="tpu_custom_call" | custom-call | tf_op jit(solution)/shard_map/pallas_call | solution.py:447
Async XLA Ops:
  0.6 48.4 %copy-start = (s32[18]{0:T(128)S(1)}, s32[18]{0:T(128)}, u32[]{:S(2)}) copy-start(s32[18]{0:T(128)} %table.1) | copy-start | bytes 220

commit v5 on v3

--- a/solution.py
+++ b/solution.py
@@ -156,12 +156,13 @@
     order = (6, 2, 5, 7, 4, 1, 3)
 
     barrier = pltpu.get_barrier_semaphore()
-    for offset in range(1, CHIPS):
+    for step in (2, 1, 3):
+        pl.semaphore_signal(barrier, inc=1, device_id={"shard": z_peer(step)}, device_id_type=MESH)
+    for offset in order:
         pl.semaphore_signal(barrier, inc=1, device_id={"dp": to(offset)}, device_id_type=MESH)
+    for step in (2, 1, 3):
+        pl.semaphore_signal(barrier, inc=1, device_id={"shard": x_peer(step)}, device_id_type=MESH)
     pl.semaphore_signal(barrier, inc=1, device_id={"dp": sibling}, device_id_type=MESH)
-    for step in range(1, 4):
-        pl.semaphore_signal(barrier, inc=1, device_id={"shard": x_peer(step)}, device_id_type=MESH)
-        pl.semaphore_signal(barrier, inc=1, device_id={"shard": z_peer(step)}, device_id_type=MESH)
 
     first_slots = ((CHIPS, tail_block, tail_other),) + tuple(
         (offset, to(offset), to(offset) + 1 - 2 * core) for offset in order + (0,)
@@ -341,12 +342,16 @@
         pass_p(offset)
     finished(x.at[rows_of(tail_other)], tails_sem)
     finished(p.at[tail_other], tailp_sem)
-    apply_at(tail_block, tail_other, source(5), source(7), source(2), source(6))
-    for offset in (4, 1, 3, 5, 7, 2, 6):
+
+    def other_here(offset):
         other = other_of(offset)
         finished(x.at[rows_of(other)], x_sems.at[CHIPS + offset])
         finished(p.at[other], p_sems.at[CHIPS + offset])
-    apply_at(*(other_of(offset) for offset in (4, 1, 3, 5, 7, 2, 6)))
+        return other
+
+    early = [other_here(offset) for offset in (4, 1, 3)]
+    apply_at(tail_block, tail_other, source(5), source(7), source(2), source(6), *early)
+    apply_at(*(other_here(offset) for offset in (5, 7, 2, 6)))
 
     keep_params.wait()
     finished(theirs, their_send)
@@ -426,7 +431,7 @@
         pltpu.make_async_copy(update_held.at[j], update.at[head], sems.at[1]).start()
         return carry
 
-    lax.fori_loop(0, count, one, 0)
+    lax.fori_loop(0, count, one, 0, unroll=3)
     pltpu.make_async_copy(new_held, new_params, sems.at[0]).wait()
     pltpu.make_async_copy(update_held, update, sems.at[1]).wait()
 

time: 53 us -> 52.8 us (level)
  no operation moved by 1% of the time
where the time goes in v5:
time: 52.8 us; the launch traced here: 52.7 us
  Pallas kernels  52.1 us (99%)
  between operations  0.65 us (1%)
    pallas_call x1, Pallas kernels, exchange(): pl.pallas_call(functools.partial(communicate, count=count, rows=rows), ou...  48.9 us
    pallas_call x1, Pallas kernels, apply(): pl.pallas_call(finish, in_specs=[pl.BlockSpec(memory_space=pltpu.SMEM), p...  3.2 us

profile of v5, /device:TPU:1, one launch (start us, length us, event | category | flops | bytes accessed | tf_op | source)
XLA Modules:
  0.0 52.7 jit_solution(14262932206946221914)
XLA Ops:
  0.6 0.0 copy-start
  0.6 48.9 %shard_map.50 = (bf16[8064,128]{1,0:T(8,128)(2,1)S(1)}, f32[8064,128]{1,0:T(8,128)S(1)}) custom-call(bf16[8064,128]{1,0:T(8,128)(2,1)} %bitcast.7, f32[8064,128]{1,0:T(8,128)} %bitcast.6), custom_call_target="tpu_custom_call" | custom-call | tf_op jit(solution)/shard_map/pallas_call | solution.py:384
  49.5 0.0 copy-done
  49.5 3.2 %shard_map.51 = (f32[18,448,128]{2,1,0:T(8,128)}, bf16[18,448,128]{2,1,0:T(8,128)(2,1)}) custom-call(s32[18]{0:T(128)S(1)} %copy-done, bf16[18,448,128]{2,1,0:T(8,128)(2,1)S(1)} %bitcast.5, f32[18,448,128]{2,1,0:T(8,128)S(1)} %bitcast.4), custom_call_target="tpu_custom_call" | custom-call | tf_op jit(solution)/shard_map/pallas_call | solution.py:441
Async XLA Ops:
  0.6 48.9 %copy-start = (s32[18]{0:T(128)S(1)}, s32[18]{0:T(128)}, u32[]{:S(2)}) copy-start(s32[18]{0:T(128)} %table.1) | copy-start | bytes 220
